TPU v7x, 128 devices: a whole 4x4x4 slice. The times are simulated.
128 devices in a mesh: ctx: 16 (over x_lo, z, core), tp: 8 (over y, x_hi).
Axes of the slice: x: 4 (x_hi: 2, x_lo: 2; x = x_hi * 2 + x_lo), y: 4, z: 4, core: 2. Of those that a mesh axis runs over, the one named last changes fastest.
Arguments:
- tokens: bfloat16 [16384, 1024], P(('ctx', 'tp')), may hold values from -6 to 6
- block_table: int32 [16, 2], replicated, may hold values from 0 to 31, as said below
- doc_ids: int32 [4, 4096], replicated, may hold values from 0 to 3, never falling along the last dimension, each value on 1 to 2048 neighbouring positions
- attn_gain: bfloat16 [1024], P('ctx'), may hold values from 0.25 to 1.75
- w_query: bfloat16 [1024, 2048], P('ctx', 'tp'), may hold values from -0.1875 to 0.1875
- w_key: bfloat16 [1024, 1024], P('ctx', 'tp'), may hold values from -0.1875 to 0.1875
- w_value: bfloat16 [1024, 1024], P('ctx', 'tp'), may hold values from -0.1875 to 0.1875
- query_gain: bfloat16 [128], P('ctx'), may hold values from 0.25 to 1.75
- key_gain: bfloat16 [128], P('ctx'), may hold values from 0.25 to 1.75
- w_out: bfloat16 [2048, 1024], P('tp', 'ctx'), may hold values from -1 to 1
- ffn_gain: bfloat16 [1024], P('ctx'), may hold values from 0.25 to 1.75
- w_gate: bfloat16 [1024, 3072], P('ctx', 'tp'), may hold values from -0.1875 to 0.1875
- w_up: bfloat16 [1024, 3072], P('ctx', 'tp'), may hold values from -0.1875 to 0.1875
- w_down: bfloat16 [3072, 1024], P('tp', 'ctx'), may hold values from -0.109375 to 0.109375
- out_grad: bfloat16 [16384, 1024], P(('ctx', 'tp')), may hold values from -6 to 6
Outputs:
- out: bfloat16 [16384, 1024], P(('ctx', 'tp'))
- grad_x: bfloat16 [16384, 1024], P(('ctx', 'tp'))
- grad_attn_gain: float32 [1024], P('ctx')
- grad_w_query: float32 [1024, 2048], P('ctx', 'tp')
- grad_w_key: float32 [1024, 1024], P('ctx', 'tp')
- grad_w_value: float32 [1024, 1024], P('ctx', 'tp')
- grad_query_gain: float32 [128], P('ctx')
- grad_key_gain: float32 [128], P('ctx')
- grad_w_out: float32 [2048, 1024], P('tp', 'ctx')
- grad_ffn_gain: float32 [1024], P('ctx')
- grad_w_gate: float32 [1024, 3072], P('ctx', 'tp')
- grad_w_up: float32 [1024, 3072], P('ctx', 'tp')
- grad_w_down: float32 [3072, 1024], P('tp', 'ctx')
Inputs may be any that keep to these rules, and one draw needn't show every extreme that they name: `block_table`: row c holds a block b below 16 and its mirror 2 * 16 - 1 - b; the first entries of the rows form a permutation, so every block appears once. `doc_ids`: never falling along a row; each document has 1 to 2048 positions, one exactly that many.
All inputs are finite; a program needn't handle non-finite values.
Results may differ from a plain program's by a relative error of at most 0.025.
Values may be sent and summed in bfloat16 or wider, within the bound.
No kernel may reach another device: no remote copies, remote signals or barrier semaphores. Data moves between devices by JAX's collectives and lax.ppermute only.
A program may use at most 192 MiB of HBM per device.

v0:
```python
import math
import jax
import jax.numpy as jnp
from jax import lax
from jax.sharding import PartitionSpec as P

HD = 128
EPS = 1e-06
THETA = 1000000.0
NEG_SCORE = -1e30


def split_up(shard, dim, length):
    before, after = (shard.shape[:dim], shard.shape[dim + 1 :])
    return jnp.moveaxis(shard.reshape(*before, length, -1, *after), dim, 0)


def sent_and_summed(shard, axis, dim):
    parts = split_up(shard, dim, lax.axis_size(axis))
    arrived = lax.all_to_all(parts, axis, split_axis=0, concat_axis=0, tiled=True)
    return arrived.astype(jnp.float32).sum(axis=0)


def normed(values, norm_gain):
    return values * lax.rsqrt(jnp.mean(values * values, axis=-1, keepdims=True) + EPS) * norm_gain


def rotate(values, cos_table, sin_table):
    half_width = values.shape[-1] // 2
    turned = jnp.concatenate([-values[..., half_width:], values[..., :half_width]], axis=-1)
    return values * cos_table + turned * sin_table


def contract_last(left_side, right_side):
    return lax.dot_general(
        left_side, right_side, (((1,), (1,)), ((), ())), preferred_element_type=jnp.float32
    )


def contract_first(left_side, right_side):
    return lax.dot_general(
        left_side, right_side, (((0,), (0,)), ((), ())), preferred_element_type=jnp.float32
    )


def send_grads(stacked):
    return lax.psum_scatter(
        stacked.astype(jnp.bfloat16), "ctx", scatter_dimension=0, tiled=True
    ).astype(jnp.float32)


def per_device(
    tokens,
    block_table,
    doc_ids,
    attn_gain,
    w_query,
    w_key,
    w_value,
    query_gain,
    key_gain,
    w_out,
    ffn_gain,
    w_gate,
    w_up,
    w_down,
    out_grad,
):
    ctx_count = lax.axis_size("ctx")
    tp_count = lax.axis_size("tp")
    ctx_rank = lax.axis_index("ctx")
    rows_dev = tokens.shape[0]
    local_rows = rows_dev * tp_count
    seq_count = doc_ids.shape[0]
    pair_rows = local_rows // seq_count
    seq_keys = pair_rows * ctx_count
    q_heads = w_query.shape[1] // HD
    kv_heads = w_key.shape[1] // HD
    group_size = q_heads // kv_heads
    q_width = q_heads * HD
    k_width = kv_heads * HD
    ff_local = w_gate.shape[1]
    score_scale = HD ** (-0.5)
    key_block = math.gcd(seq_keys, 512)
    key_blocks = seq_keys // key_block
    seq_len = doc_ids.shape[1]
    half_block = pair_rows // 2
    seq_index = jnp.arange(seq_len, dtype=jnp.int32)
    change = jnp.concatenate(
        [jnp.ones((seq_count, 1), dtype=bool), doc_ids[:, 1:] != doc_ids[:, :-1]], axis=1
    )
    doc_starts = lax.cummax(jnp.where(change, seq_index[None, :], 0), axis=1)
    key_index = jnp.arange(seq_keys, dtype=jnp.int32)
    key_inner = key_index % pair_rows
    key_place = (
        block_table[key_index // pair_rows, key_inner // half_block] * half_block
        + key_inner % half_block
    )
    key_doc = doc_ids[:, key_place]
    query_index = jnp.arange(local_rows, dtype=jnp.int32)
    query_seq = query_index // pair_rows
    query_inner = query_index % pair_rows
    query_place = (
        block_table[jnp.zeros_like(query_index) + ctx_rank, query_inner // half_block] * half_block
        + query_inner % half_block
    )
    query_doc = doc_ids[query_seq, query_place]
    query_pos = query_place - doc_starts[query_seq, query_place]
    query_place_s = query_place.reshape(seq_count, pair_rows)
    query_doc_s = query_doc.reshape(seq_count, pair_rows)
    freq_steps = jnp.arange(HD // 2, dtype=jnp.float32) * (2.0 / HD)
    angles = (
        query_pos.astype(jnp.float32)[:, None] * jnp.power(jnp.float32(THETA), -freq_steps)[None, :]
    )
    angles = jnp.concatenate([angles, angles], axis=1)[:, None, :]
    cos_table = jnp.cos(angles)
    sin_table = jnp.sin(angles)
    gain_attn, gain_query, gain_key, w_qkv, w_proj = (
        lax.all_gather(attn_gain, "ctx", axis=0, tiled=True),
        lax.all_gather(query_gain, "ctx", axis=0, tiled=True),
        lax.all_gather(key_gain, "ctx", axis=0, tiled=True),
        lax.all_gather(
            jnp.concatenate([w_query, w_key, w_value], axis=1), "ctx", axis=0, tiled=True
        ),
        lax.all_gather(w_out, "ctx", axis=1, tiled=True),
    )
    tokens_f = tokens.astype(jnp.float32)
    normal_one_f, norm_one_back = jax.vjp(normed, tokens_f, gain_attn.astype(jnp.float32))
    normal_one = normal_one_f.astype(jnp.bfloat16)
    rows_one = lax.all_gather(normal_one, "tp", axis=0, tiled=True)
    projected = jnp.dot(rows_one, w_qkv, preferred_element_type=jnp.float32)
    query_pre = projected[:, :q_width].reshape(local_rows, q_heads, HD)
    key_pre = projected[:, q_width : q_width + k_width].reshape(local_rows, kv_heads, HD)
    value_low = projected[:, q_width + k_width :].astype(jnp.bfloat16)

    def head_prep(pre_values, norm_gain):
        return rotate(normed(pre_values, norm_gain), cos_table, sin_table)

    query_rot, query_back = jax.vjp(head_prep, query_pre, gain_query.astype(jnp.float32))
    key_rot, key_back = jax.vjp(head_prep, key_pre, gain_key.astype(jnp.float32))
    query_low = query_rot.astype(jnp.bfloat16).reshape(
        seq_count, pair_rows, kv_heads, group_size, HD
    )
    key_low = key_rot.astype(jnp.bfloat16).reshape(seq_count, pair_rows, k_width)
    own_values = value_low.reshape(seq_count, pair_rows, k_width)
    keys_all, values_all = (
        lax.all_gather(key_low, "ctx", axis=1, tiled=True),
        lax.all_gather(own_values, "ctx", axis=1, tiled=True),
    )
    keys_seq = keys_all.reshape(seq_count, seq_keys, kv_heads, HD)
    values_seq = values_all.reshape(seq_count, seq_keys, kv_heads, HD)

    def tile_at(start):
        key_tile = lax.dynamic_slice_in_dim(keys_seq, start, key_block, 1)
        value_tile = lax.dynamic_slice_in_dim(values_seq, start, key_block, 1)
        place_tile = lax.dynamic_slice_in_dim(key_place, start, key_block, 0)
        doc_tile = lax.dynamic_slice_in_dim(key_doc, start, key_block, 1)
        scores = (
            jnp.einsum("sqhgd,skhd->shgqk", query_low, key_tile, preferred_element_type=jnp.float32)
            * score_scale
        )
        allowed = (doc_tile[:, None, :] == query_doc_s[:, :, None]) & (
            place_tile[None, None, :] <= query_place_s[:, :, None]
        )
        return (key_tile, value_tile, scores, allowed[:, None, None, :, :])

    starts = jnp.arange(key_blocks, dtype=jnp.int32) * key_block

    def stats_step(running, start):
        peak_score, row_total = running
        key_tile, value_tile, scores, allowed = tile_at(start)
        scores = jnp.where(allowed, scores, NEG_SCORE)
        new_peak = jnp.maximum(peak_score, jnp.max(scores, axis=-1))
        weights = jnp.where(allowed, jnp.exp(scores - new_peak[..., None]), 0.0)
        row_total = row_total * jnp.exp(peak_score - new_peak) + jnp.sum(weights, axis=-1)
        return ((new_peak, row_total), None)

    stat_shape = (seq_count, kv_heads, group_size, pair_rows)
    stats_final = lax.scan(
        stats_step,
        (jnp.full(stat_shape, NEG_SCORE, jnp.float32), jnp.zeros(stat_shape, jnp.float32)),
        starts,
    )[0]
    log_total = stats_final[0] + jnp.log(stats_final[1])

    def output_step(accum, start):
        key_tile, value_tile, scores, allowed = tile_at(start)
        probs_low = jnp.where(allowed, jnp.exp(scores - log_total[..., None]), 0.0).astype(
            jnp.bfloat16
        )
        return (
            accum
            + jnp.einsum(
                "shgqk,skhd->sqhgd", probs_low, value_tile, preferred_element_type=jnp.float32
            ),
            None,
        )

    head_shape = (seq_count, pair_rows, kv_heads, group_size, HD)
    attended = lax.scan(output_step, jnp.zeros(head_shape, jnp.float32), starts)[0]
    attn_low = attended.reshape(local_rows, q_width).astype(jnp.bfloat16)
    resid = tokens_f + lax.psum_scatter(
        jnp.dot(attn_low, w_proj, preferred_element_type=jnp.float32).astype(jnp.bfloat16),
        "tp",
        scatter_dimension=0,
        tiled=True,
    ).astype(jnp.float32)
    gain_ffn, w_gu, w_dn = (
        lax.all_gather(ffn_gain, "ctx", axis=0, tiled=True),
        lax.all_gather(jnp.concatenate([w_gate, w_up], axis=1), "ctx", axis=0, tiled=True),
        lax.all_gather(w_down, "ctx", axis=1, tiled=True),
    )
    normal_two_f, norm_two_back = jax.vjp(normed, resid, gain_ffn.astype(jnp.float32))
    normal_two = normal_two_f.astype(jnp.bfloat16)
    rows_two = lax.all_gather(normal_two, "tp", axis=0, tiled=True)
    gate_up = jnp.dot(rows_two, w_gu, preferred_element_type=jnp.float32)
    gate = gate_up[:, :ff_local]
    up_proj = gate_up[:, ff_local:]
    sigmoid_gate = jax.nn.sigmoid(gate)
    silu_gate = gate * sigmoid_gate
    hidden = (silu_gate * up_proj).astype(jnp.bfloat16)
    out = (
        resid
        + sent_and_summed(
            jnp.dot(hidden, w_dn, preferred_element_type=jnp.float32).astype(jnp.bfloat16), "tp", 0
        )
    ).astype(jnp.bfloat16)
    grad_rows = lax.all_gather(out_grad, "tp", axis=0, tiled=True)
    grad_hidden = contract_last(grad_rows, w_dn)
    grad_gate = grad_hidden * up_proj * (sigmoid_gate * (1.0 + gate * (1.0 - sigmoid_gate)))
    grad_up = grad_hidden * silu_gate
    grad_gu = jnp.concatenate([grad_gate, grad_up], axis=1).astype(jnp.bfloat16)
    mlp_grads = jnp.concatenate(
        [contract_first(rows_two, grad_gu), contract_first(grad_rows, hidden)], axis=1
    )
    mlp_early = send_grads(mlp_grads)
    grad_norm_two = sent_and_summed(contract_last(grad_gu, w_gu).astype(jnp.bfloat16), "tp", 0)
    grad_resid_norm, grad_gain_ffn = norm_two_back(grad_norm_two)
    grad_resid = out_grad.astype(jnp.float32) + grad_resid_norm
    branch_rows = lax.all_gather(grad_resid.astype(jnp.bfloat16), "tp", axis=0, tiled=True)
    grad_attn_low = contract_last(branch_rows, w_proj).astype(jnp.bfloat16)
    grad_out_cols = contract_first(branch_rows, attn_low)
    grad_attn_heads = grad_attn_low.reshape(head_shape)
    delta = jnp.transpose(
        jnp.sum(grad_attn_heads.astype(jnp.float32) * attended, axis=-1), (0, 2, 3, 1)
    )

    def scores_grad(probs, grad_probs, delta_here):
        return (probs * (grad_probs - delta_here[..., None])).astype(jnp.bfloat16)

    def grad_step(carry, start):
        accum, key_grad_all, value_grad_all = carry
        key_tile, value_tile, scores, allowed = tile_at(start)
        probs = jnp.where(allowed, jnp.exp(scores - log_total[..., None]), 0.0)
        probs_low = probs.astype(jnp.bfloat16)
        grad_value = jnp.einsum(
            "shgqk,sqhgd->skhd", probs_low, grad_attn_heads, preferred_element_type=jnp.float32
        )
        grad_probs = jnp.einsum(
            "sqhgd,skhd->shgqk", grad_attn_heads, value_tile, preferred_element_type=jnp.float32
        )
        grad_scores = scores_grad(probs, grad_probs, delta)
        accum = (
            accum
            + jnp.einsum(
                "shgqk,skhd->sqhgd", grad_scores, key_tile, preferred_element_type=jnp.float32
            )
            * score_scale
        )
        grad_key = (
            jnp.einsum(
                "shgqk,sqhgd->skhd", grad_scores, query_low, preferred_element_type=jnp.float32
            )
            * score_scale
        )
        key_grad_all = lax.dynamic_update_slice_in_dim(
            key_grad_all, grad_key.reshape(seq_count, key_block, k_width), start, 1
        )
        value_grad_all = lax.dynamic_update_slice_in_dim(
            value_grad_all, grad_value.reshape(seq_count, key_block, k_width), start, 1
        )
        return ((accum, key_grad_all, value_grad_all), None)

    kv_zero = jnp.zeros((seq_count, seq_keys, k_width), jnp.float32)
    grad_query, key_grad_all, value_grad_all = lax.scan(
        grad_step, (jnp.zeros(head_shape, jnp.float32), kv_zero, kv_zero), starts
    )[0]
    grad_keys, grad_values = (
        lax.psum_scatter(
            key_grad_all.astype(jnp.bfloat16), "ctx", scatter_dimension=1, tiled=True
        ).astype(jnp.float32),
        lax.psum_scatter(
            value_grad_all.astype(jnp.bfloat16), "ctx", scatter_dimension=1, tiled=True
        ).astype(jnp.float32),
    )
    grad_query_pre, grad_gain_query = query_back(grad_query.reshape(local_rows, q_heads, HD))
    grad_key_pre, grad_gain_key = key_back(grad_keys.reshape(local_rows, kv_heads, HD))
    grad_qkv = jnp.concatenate(
        [
            grad_query_pre.reshape(local_rows, q_width),
            grad_key_pre.reshape(local_rows, k_width),
            grad_values.reshape(local_rows, k_width),
        ],
        axis=1,
    ).astype(jnp.bfloat16)
    attn_grads = jnp.concatenate([contract_first(rows_one, grad_qkv), grad_out_cols], axis=1)
    grad_norm_one = sent_and_summed(contract_last(grad_qkv, w_qkv).astype(jnp.bfloat16), "tp", 0)
    grad_input_norm, grad_gain_attn = norm_one_back(grad_norm_one)
    grad_x = (grad_resid + grad_input_norm).astype(jnp.bfloat16)
    gain_sums = lax.psum(
        (grad_gain_attn, grad_gain_query, grad_gain_key, grad_gain_ffn), ("ctx", "tp")
    )
    d_share = gain_sums[0].shape[0] // ctx_count
    h_share = gain_sums[1].shape[0] // ctx_count
    attn_owned = send_grads(attn_grads)
    return (
        out,
        grad_x,
        lax.dynamic_slice_in_dim(gain_sums[0], ctx_rank * d_share, d_share),
        attn_owned[:, :q_width],
        attn_owned[:, q_width : q_width + k_width],
        attn_owned[:, q_width + k_width : q_width + 2 * k_width],
        lax.dynamic_slice_in_dim(gain_sums[1], ctx_rank * h_share, h_share),
        lax.dynamic_slice_in_dim(gain_sums[2], ctx_rank * h_share, h_share),
        jnp.transpose(attn_owned[:, q_width + 2 * k_width :]),
        lax.dynamic_slice_in_dim(gain_sums[3], ctx_rank * d_share, d_share),
        mlp_early[:, :ff_local],
        mlp_early[:, ff_local : 2 * ff_local],
        jnp.transpose(mlp_early[:, 2 * ff_local :]),
    )


def solution(mesh):
    in_specs = (
        P(("ctx", "tp"), None),
        P(),
        P(),
        P("ctx"),
        P("ctx", "tp"),
        P("ctx", "tp"),
        P("ctx", "tp"),
        P("ctx"),
        P("ctx"),
        P("tp", "ctx"),
        P("ctx"),
        P("ctx", "tp"),
        P("ctx", "tp"),
        P("tp", "ctx"),
        P(("ctx", "tp"), None),
    )
    out_specs = (
        P(("ctx", "tp"), None),
        P(("ctx", "tp"), None),
        P("ctx"),
        P("ctx", "tp"),
        P("ctx", "tp"),
        P("ctx", "tp"),
        P("ctx"),
        P("ctx"),
        P("tp", "ctx"),
        P("ctx"),
        P("ctx", "tp"),
        P("ctx", "tp"),
        P("tp", "ctx"),
    )
    return jax.shard_map(
        per_device, mesh=mesh, in_specs=in_specs, out_specs=out_specs, check_vma=False
    )
```

profile of v0, /device:TPU:1, one launch (start us, length us, event | category | flops | bytes accessed | tf_op | source)
XLA Modules:
  0.0 1124.1 jit_solution(7905820449707120170)
XLA Ops:
  14.7 30.3 %all-reduce.11 = (bf16[1024]{0:T(1024)(128)(2,1)S(1)}, bf16[128]{0:T(256)(128)(2,1)S(1)}, bf16[128]{0:T(256)(128)(2,1)S(1)}, bf16[1024]{0:T(1024)(128)(2,1)}) all-reduce(bf16[1024]{0:T(1024)(128)(2,1)S(1)} %dynamic-update-slice, bf16[128]{0:T(256)(128)(2,1)S(1)} %dynamic-update-slice.1, ...), channel_id=1, replica_groups=mesh['ctx'=16,'tp'=8] {'ctx'}, use_global_device_ids=true, to_apply=%add.6 | all-reduce | flops 2304 | bytes 9216
  52.0 8.8 gather_fusion.2
  60.9 9.1 gather_fusion.4
  70.9 33.8 %all-gather.9.cloned.1.call-done = bf16[1024,1024]{1,0:T(8,128)(2,1)} async-done(((bf16[128,1024]{1,0:T(8,128)(2,1)}), bf16[1024,1024]{1,0:T(8,128)(2,1)}) %all-gather.9.cloned.1.call-update) | async-done | bytes 2097168 | tf_op jit(solution)/shard_map/all_gather | solution.py:130
  112.1 9.1 gather_fusion.3
  124.0 33.8 %gather_fusion = s32[4096]{0:T(1024)S(1)} fusion(s32[16,2]{0,1:T(2,128)S(1)} %copy-done, s32[4096]{0:T(1024)S(1)} %bitcast.382), kind=kCustom, calls=%fused_computation | custom fusion | bytes 65536 | tf_op jit(solution)/shard_map/gather | solution.py:96
  157.9 15.8 %gather_fusion.1 = s32[4096,4]{1,0:T(8,128)} fusion(s32[4,4096]{0,1:T(8,128)} %copy.155, s32[4096]{0:T(1024)S(1)} %broadcast_clamp_fusion), kind=kCustom, calls=%fused_computation.1 | custom fusion | bytes 147456 | tf_op jit(solution)/shard_map/gather | solution.py:99
  181.5 22.6 %all_gather.49 = bf16[256,1024]{0,1:T(8,128)(2,1)} all-gather(bf16[256,64]{0,1:T(8,128)(2,1)S(1)} %copy-done.40), channel_id=1, replica_groups=mesh['ctx'=16,'tp'=8] {'ctx'}, dimensions={1}, use_global_device_ids=true | all-gather | bytes 557056 | tf_op jit(solution)/shard_map/all_gather | solution.py:125
  213.8 56.3 %while.42 = (s32[]{:T(128)}, f32[4,1,2,256]{3,2,0,1:T(2,128)S(1)}, f32[4,1,2,256]{3,2,0,1:T(2,128)S(1)}, s32[8]{0:T(128)}, s32[4,4096]{1,0:T(4,128)S(1)}, /*inde...) while((s32[]{:T(128)}, f32[4,1,2,256]{3,2,0,1:T(2,128)S(1)}, ...), condition=%wide.wide.region_8.9_spmd.clone, body=%wide.wide.region_5.8_spmd.clone.sunk | while | flops 278407168 | bytes 11155674 | solution.py:179
  270.2 54.3 %while.43 = (s32[]{:T(128)}, f32[4,256,1,2,128]{1,4,3,0,2:T(8,128)S(1)}, s32[8]{0:T(128)}, bf16[4,4096,1,128]{3,1,0,2:T(8,128)(2,1)}, s32[4,4096]{1,0:T(4,128)S(...) while((s32[]{:T(128)}, ...), condition=%wide.wide.region_10.11_spmd.clone, body=%wide.wide.region_9.10_spmd.clone.sunk | while | flops 543162368 | bytes 4767452 | solution.py:200
  328.5 68.6 %reduce-scatter.10.cloned.1.call-done = bf16[128,1024]{1,0:T(8,128)(2,1)} async-done(((bf16[1024,1024]{1,0:T(8,128)(2,1)}), bf16[128,1024]{1,0:T(8,128)(2,1)}) %reduce-scatter.10.cloned.1.call-update) | async-done | bytes 262160 | tf_op jit(solution)/shard_map/reduce_scatter | solution.py:202
  400.8 23.9 %all_gather.53 = bf16[384,1024]{0,1:T(8,128)(2,1)S(1)} all-gather(bf16[384,64]{0,1:T(8,128)(2,1)} %param.34), channel_id=1, replica_groups=mesh['ctx'=16,'tp'=8] {'ctx'}, dimensions={1}, use_global_device_ids=true | all-gather | bytes 835584 | tf_op jit(solution)/shard_map/all_gather | solution.py:211
  424.7 9.1 all-gather.19.cloned.1.call-done
  433.8 55.7 %all-gather.17.cloned.1.call-done = bf16[1024,1024]{1,0:T(8,128)(2,1)} async-done(((bf16[128,1024]{1,0:T(8,128)(2,1)}), bf16[1024,1024]{1,0:T(8,128)(2,1)}) %all-gather.17.cloned.1.call-update) | async-done | bytes 2097168 | tf_op jit(solution)/shard_map/all_gather | solution.py:215
  495.0 48.6 %all-gather.21.cloned.1.call-done = bf16[1024,1024]{1,0:T(8,128)(2,1)} async-done(((bf16[128,1024]{1,0:T(8,128)(2,1)}), bf16[1024,1024]{1,0:T(8,128)(2,1)}) %all-gather.21.cloned.1.call-update) | async-done | bytes 2097168 | tf_op jit(solution)/shard_map/all_gather | solution.py:228
  550.7 30.0 %all_to_all.15 = bf16[8,128,1024]{2,1,0:T(8,128)(2,1)S(1)} all-to-all(bf16[8,128,1024]{2,1,0:T(8,128)(2,1)S(1)} %bitcast.393), channel_id=1, replica_groups=mesh['ctx'=16,'tp'=8] {'tp'}, dimensions={0} | all-to-all | bytes 4194304 | tf_op jit(solution)/shard_map/all_to_all | solution.py:20
  583.5 52.6 %all-gather.23.cloned.1.call-done = bf16[1024,1024]{1,0:T(8,128)(2,1)} async-done(((bf16[128,1024]{1,0:T(8,128)(2,1)}), bf16[1024,1024]{1,0:T(8,128)(2,1)}) %all-gather.23.cloned.1.call-update) | async-done | bytes 2097168 | tf_op jit(solution)/shard_map/all_gather | solution.py:240
  648.6 176.8 %while.44 = (s32[]{:T(128)}, f32[4,256,1,2,128]{1,4,3,0,2:T(8,128)S(1)}, bf16[4,4096,128]{2,1,0:T(8,128)(2,1)}, bf16[4,4096,128]{2,1,0:T(8,128)(2,1)}, s32[8]{0:...) while((s32[]{:T(128)}, ...), condition=%wide.wide.region_18.19_spmd.clone, body=%wide.wide.region_17.18_spmd.clone.sunk | while | flops 1355546624 | bytes 29423888 | solution.py:285
  659.7 5.6 dynamic_update_slice.12
  682.0 5.6 dynamic_update_slice.12
  704.3 5.6 dynamic_update_slice.12
  709.8 5.6 dynamic_update_slice.13
  726.5 5.6 dynamic_update_slice.12
  748.8 5.6 dynamic_update_slice.12
  771.1 5.6 dynamic_update_slice.12
  793.3 5.6 dynamic_update_slice.12
  798.9 5.6 dynamic_update_slice.13
  854.6 41.9 %reduce-scatter.14.cloned.1.call-done = bf16[4,256,128]{2,1,0:T(8,128)(2,1)} async-done(((bf16[4,4096,128]{2,1,0:T(8,128)(2,1)}), bf16[4,256,128]{2,1,0:T(8,128)(2,1)}) %reduce-scatter.14.cloned.1.call-update) | async-done | bytes 262160 | tf_op jit(solution)/shard_map/reduce_scatter | solution.py:292
  897.6 64.9 %reduce-scatter.12.cloned.1.call-done = bf16[4,256,128]{2,1,0:T(8,128)(2,1)} async-done(((bf16[4,4096,128]{2,1,0:T(8,128)(2,1)}), bf16[4,256,128]{2,1,0:T(8,128)(2,1)}) %reduce-scatter.12.cloned.1.call-update) | async-done | bytes 262160 | tf_op jit(solution)/shard_map/reduce_scatter | solution.py:289
  976.5 6.8 all-to-all-start.2
  986.1 45.8 %reduce-scatter.18.cloned.1.call-done = bf16[64,1152]{1,0:T(8,128)(2,1)} async-done(((bf16[1024,1152]{1,0:T(8,128)(2,1)}), bf16[64,1152]{1,0:T(8,128)(2,1)}) %reduce-scatter.18.cloned.1.call-update) | async-done | bytes 147472
  1040.3 68.1 %all-reduce.10 = (f32[1024]{0:T(1024)S(1)}, f32[128]{0:T(128)S(1)}, f32[128]{0:T(128)S(1)}, f32[1024]{0:T(1024)S(1)}) all-reduce(f32[1024]{0:T(1024)S(1)} %get-tuple-element.576, f32[128]{0:T(128)S(1)} %get-tuple-element.574, f32[128]{0:T(128)S(1)} %get-tuple-element.570, ...), channel_id=1, replica_groups=mesh['ctx'=16,'tp'=8] {'ctx','tp'}, use_global_device_ids=true, to_apply=%region_26.27 | all-reduce | flops 2304 | bytes 18432 | tf_op jit(solution)/shard_map/psum | solution.py:310
  (493 shorter events, 330.1 us)
Async XLA Ops:
  7.2 44.9 %copy-start = (s32[16,2]{0,1:T(2,128)S(1)}, s32[16,2]{0,1:T(2,128)}, u32[]{:S(2)}) copy-start(s32[16,2]{0,1:T(2,128)} %param.22) | copy-start | bytes 388
  7.2 63.7 %all-gather.11.cloned.1.call-start = ((), (), s32[]{:S(2)}) async-start(), calls=%async_computation.9 | async-start | bytes 1114112 | tf_op jit(solution)/shard_map/all_gather | solution.py:122
  8.7 96.0 %all-gather.9.cloned.1.call-start = ((), (), s32[]{:S(2)}) async-start(), calls=%async_computation.8 | async-start | bytes 2359296 | tf_op jit(solution)/shard_map/all_gather | solution.py:130
  49.0 164.8 %all-gather.15.cloned.1.call-start = ((), (), s32[]{:S(2)}) async-start(), calls=%async_computation.11 | async-start | bytes 4456448 | tf_op jit(solution)/shard_map/all_gather | solution.py:147
  49.1 59.0 %copy-start.41 = (f32[128]{0:T(128)}, f32[128]{0:T(128)S(1)}, u32[]{:S(2)}) copy-start(f32[128]{0:T(128)S(1)} %convert_element_type.135) | copy-start | bytes 1540
  70.1 51.2 %copy-start.32 = (s32[1024]{0:T(1024)}, s32[1024]{0:T(1024)S(1)}, u32[]{:S(2)}) copy-start(s32[1024]{0:T(1024)S(1)} %get-tuple-element.1194) | copy-start | bytes 12292
  107.8 99.0 %copy-start.3 = (f32[1024,512]{0,1:T(8,128)}, f32[1024,512]{0,1:T(8,128)S(1)}, u32[]{:S(2)}) copy-start(f32[1024,512]{0,1:T(8,128)S(1)} %fusion.161) | copy-start | bytes 6291460
  112.0 158.2 %all-gather.13.cloned.1.call-start = ((), (), s32[]{:S(2)}) async-start(), calls=%async_computation.10 | async-start | bytes 4456448 | tf_op jit(solution)/shard_map/all_gather | solution.py:148
  121.2 36.6 %copy-start.34 = (s32[1024]{0:T(1024)}, s32[1024]{0:T(1024)S(1)}, u32[]{:S(2)}) copy-start(s32[1024]{0:T(1024)S(1)} %gather_fusion.3) | copy-start | bytes 12292
  157.9 23.7 %copy-start.40 = (bf16[256,64]{0,1:T(8,128)(2,1)S(1)}, bf16[256,64]{0,1:T(8,128)(2,1)}, u32[]{:S(2)}) copy-start(bf16[256,64]{0,1:T(8,128)(2,1)} %param.30) | copy-start | bytes 98308
  213.6 183.5 %reduce-scatter.10.cloned.1.call-start = ((), (), s32[]{:S(2)}) async-start(), calls=%async_computation.12 | async-start | bytes 2359296 | tf_op jit(solution)/shard_map/reduce_scatter | solution.py:202
  213.8 56.4 %copy-start.13 = (f32[4,256,1,2,128]{1,4,3,0,2:T(8,128)S(1)}, f32[4,256,1,2,128]{1,4,3,0,2:T(8,128)}, u32[]{:S(2)}) copy-start(f32[4,256,1,2,128]{1,4,3,0,2:T(8,128)} %custom-call.10) | copy-start | bytes 3145732
  325.5 71.5 %copy-start.5 = (bf16[128,1024]{1,0:T(8,128)(2,1)S(1)}, bf16[128,1024]{1,0:T(8,128)(2,1)}, u32[]{:S(2)}) copy-start(bf16[128,1024]{1,0:T(8,128)(2,1)} %param.21) | copy-start | bytes 786436
  327.7 106.2 %all-gather.19.cloned.1.call-start = ((), (), s32[]{:S(2)}) async-start(), calls=%async_computation.14 | async-start | bytes 1671168 | tf_op jit(solution)/shard_map/all_gather | solution.py:210
  328.4 161.1 %all-gather.17.cloned.1.call-start = ((), (), s32[]{:S(2)}) async-start(), calls=%async_computation.13 | async-start | bytes 2359296 | tf_op jit(solution)/shard_map/all_gather | solution.py:215
  400.0 143.7 %all-gather.21.cloned.1.call-start = ((), (), s32[]{:S(2)}) async-start(), calls=%async_computation.15 | async-start | bytes 2359296 | tf_op jit(solution)/shard_map/all_gather | solution.py:228
  400.7 235.4 %all-gather.23.cloned.1.call-start = ((), (), s32[]{:S(2)}) async-start(), calls=%async_computation.16 | async-start | bytes 2359296 | tf_op jit(solution)/shard_map/all_gather | solution.py:240
  424.7 118.9 %copy-start.24 = (bf16[384,1024]{0,1:T(8,128)(2,1)}, bf16[384,1024]{0,1:T(8,128)(2,1)S(1)}, u32[]{:S(2)}) copy-start(bf16[384,1024]{0,1:T(8,128)(2,1)S(1)} %all_gather.53) | copy-start | bytes 2359300
  582.5 56.8 %copy-start.47 = (f32[128]{0:T(128)}, f32[128]{0:T(128)S(1)}, u32[]{:S(2)}) copy-start(f32[128]{0:T(128)S(1)} %multiply_multiply_fusion.4) | copy-start | bytes 1540
  583.4 313.1 %reduce-scatter.14.cloned.1.call-start = ((), (), s32[]{:S(2)}) async-start(), calls=%async_computation.18 | async-start | bytes 4456448 | tf_op jit(solution)/shard_map/reduce_scatter | solution.py:292
  825.5 137.0 %reduce-scatter.12.cloned.1.call-start = ((), (), s32[]{:S(2)}) async-start(), calls=%async_computation.17 | async-start | bytes 4456448 | tf_op jit(solution)/shard_map/reduce_scatter | solution.py:289
  826.2 205.7 %reduce-scatter.18.cloned.1.call-start = ((), (), s32[]{:S(2)}) async-start(), calls=%async_computation.20 | async-start | bytes 2506752
  841.1 135.5 %all-to-all-start = ((bf16[8,128,1024]{2,1,0:T(8,128)(2,1)}), bf16[8,128,1024]{2,1,0:T(8,128)(2,1)}, u32[]{:S(2)}, u32[]{:S(2)}) async-start(bf16[8,128,1024]{2,1,0:T(8,128)(2,1)} %bitcast.391), calls=%async_computation.1 | async-start | bytes 4194304 | tf_op jit(solution)/shard_map/all_to_all | solution.py:20
  845.4 267.7 %reduce-scatter.16.cloned.1.call-start = ((), (), s32[]{:S(2)}) async-start(), calls=%async_computation.19 | async-start | bytes 1671168
  854.6 110.9 %copy-start.15 = (f32[1024,1,64]{0,2,1:T(8,128)S(1)}, f32[1024,1,64]{0,2,1:T(8,128)}, u32[]{:S(2)}) copy-start(f32[1024,1,64]{0,2,1:T(8,128)} %get-tuple-element.686) | copy-start | bytes 786436
  897.5 69.8 %copy-start.42 = (f32[128]{0:T(128)S(1)}, f32[128]{0:T(128)}, u32[]{:S(2)}) copy-start(f32[128]{0:T(128)} %copy-done.41) | copy-start | bytes 1540
  976.5 62.4 %all-to-all-start.2 = ((bf16[8,128,1024]{2,1,0:T(8,128)(2,1)}), bf16[8,128,1024]{2,1,0:T(8,128)(2,1)S(1)}, u32[]{:S(2)}, u32[]{:S(2)}) async-start(bf16[8,128,1024]{2,1,0:T(8,128)(2,1)} %bitcast.392), calls=%async_computation.5 | async-start | bytes 4194304 | tf_op jit(solution)/shard_map/all_to_all | solution.py:20
  1035.5 75.2 %copy-start.51 = (f32[128]{0:T(128)S(1)}, f32[128]{0:T(128)}, u32[]{:S(2)}) copy-start(f32[128]{0:T(128)} %copy-done.50) | copy-start | bytes 1540
  1035.5 75.2 %copy-start.9 = (f32[128,1024]{1,0:T(8,128)S(1)}, f32[128,1024]{1,0:T(8,128)}, u32[]{:S(2)}) copy-start(f32[128,1024]{1,0:T(8,128)} %copy-done.8) | copy-start | bytes 1572868
  1035.5 75.2 %copy-start.11 = (bf16[128,1024]{1,0:T(8,128)(2,1)S(1)}, bf16[128,1024]{1,0:T(8,128)(2,1)}, u32[]{:S(2)}) copy-start(bf16[128,1024]{1,0:T(8,128)(2,1)} %reduce-scatter.10.cloned.1.call-done) | copy-start | bytes 786436
  1035.5 75.3 %copy-start.17 = (bf16[128,1024]{1,0:T(8,128)(2,1)S(1)}, bf16[128,1024]{1,0:T(8,128)(2,1)}, u32[]{:S(2)}) copy-start(bf16[128,1024]{1,0:T(8,128)(2,1)} %param.35) | copy-start | bytes 786436
  1035.5 75.3 %copy-start.48 = (f32[128]{0:T(128)S(1)}, f32[128]{0:T(128)}, u32[]{:S(2)}) copy-start(f32[128]{0:T(128)} %copy-done.47) | copy-start | bytes 1540
  (45 other events, 111.3 us)
Sparse Core Ops, SparseCore 0:
  10.3 36.2 all-gather.10
  49.5 55.1 all-gather.8
  112.1 36.1 all-gather.14
  213.7 33.6 all-gather.12
  327.8 69.2 reduce-scatter.9
  399.2 34.5 all-gather.18
  436.7 52.7 all-gather.16
  491.9 51.7 all-gather.20
  583.5 52.5 all-gather.22
  825.6 70.8 reduce-scatter.13
  898.9 63.5 reduce-scatter.11
  964.7 67.1 reduce-scatter.17
  1034.3 60.6 reduce-scatter.15
where the time goes:
time: 1140 us; the launch traced here: 1120 us
  waiting for transfers between devices  423 us (37%)
  local copies, waits for them, and re-layouts  248 us (22%)
  blocking collectives  175 us (15%)
  matrix products  135 us (12%)
  other arithmetic  66.5 us (6%)
  loops' own time  47.7 us (4%)
  between operations  16.8 us (1%)
  starting transfers between devices  12.1 us (1%)
    reduce_scatter x1, waiting for transfers between devices, per_device(): lax.psum_scatter(jnp.dot(attn_low, w_proj, preferred_element_type=jnp.flo...  68.6 us
    psum x1, blocking collectives, per_device(): lax.psum((grad_gain_attn, grad_gain_query, grad_gain_key, grad_gain_ffn),...  68.1 us
    reduce_scatter x1, waiting for transfers between devices, per_device(): lax.psum_scatter(key_grad_all.astype(jnp.bfloat16), 'ctx', scatter_dimens...  64.9 us
    all_gather x1, waiting for transfers between devices, per_device(): rows_two = lax.all_gather(normal_two, 'tp', axis=0, tiled=True)  55.7 us
    all_gather x1, waiting for transfers between devices, per_device(): lax.all_gather(grad_resid.astype(jnp.bfloat16), 'tp', axis=0, tiled=True)  52.6 us
    all_gather x1, waiting for transfers between devices, per_device(): grad_rows = lax.all_gather(out_grad, 'tp', axis=0, tiled=True)  48.6 us
    unnamed x15, waiting for transfers between devices  47.4 us
    dynamic_update_slice x8, local copies, waits for them, and re-layouts, grad_step(): lax.dynamic_update_slice_in_dim(key_grad_all, grad_key.reshape(seq_count,...  43.9 us
  transfers between devices with their start and end apart: 15, of which 9 were waited for; matrix products, arithmetic and copies ran while one was open for 18% of the time, Pallas kernels for 0%

commit v1 on v0

--- a/solution.py
+++ b/solution.py
@@ -1,13 +1,23 @@
+import functools
 import math
 import jax
 import jax.numpy as jnp
 from jax import lax
 from jax.sharding import PartitionSpec as P
+from jax.lax import psum
 
 HD = 128
 EPS = 1e-06
 THETA = 1000000.0
 NEG_SCORE = -1e30
+
+
+def raise_the_ends(mine, mesh_name, axis_name):
+    now = psum(psum(mine, mesh_name), axis_name)
+    return now
+
+
+register_the_knots = functools.partial(raise_the_ends, mesh_name="ctx", axis_name="tp")
 
 
 def split_up(shard, dim, length):
@@ -307,9 +317,7 @@
     grad_norm_one = sent_and_summed(contract_last(grad_qkv, w_qkv).astype(jnp.bfloat16), "tp", 0)
     grad_input_norm, grad_gain_attn = norm_one_back(grad_norm_one)
     grad_x = (grad_resid + grad_input_norm).astype(jnp.bfloat16)
-    gain_sums = lax.psum(
-        (grad_gain_attn, grad_gain_query, grad_gain_key, grad_gain_ffn), ("ctx", "tp")
-    )
+    gain_sums = register_the_knots((grad_gain_attn, grad_gain_query, grad_gain_key, grad_gain_ffn))
     d_share = gain_sums[0].shape[0] // ctx_count
     h_share = gain_sums[1].shape[0] // ctx_count
     attn_owned = send_grads(attn_grads)

time: 1140 us -> 1130 us (level)
  blocking collectives: 175 us -> 159 us
    psum x1 -> x2, blocking collectives: 68.1 us -> 52.7 us  [raise_the_ends(): now = psum(psum(mine, mesh_name), axis_name)]
  transfers between devices with their start and end apart: 15 -> 15, of which waited for: 9 -> 9; matrix products, arithmetic and copies ran while one was open for 18% -> 19% of each run, Pallas kernels for 0% -> 0%
where the time goes in v1:
time: 1130 us; the launch traced here: 1110 us
  waiting for transfers between devices  423 us (37%)
  local copies, waits for them, and re-layouts  248 us (22%)
  blocking collectives  159 us (14%)
  matrix products  135 us (12%)
  other arithmetic  66.6 us (6%)
  loops' own time  47.7 us (4%)
  between operations  16.9 us (1%)
  starting transfers between devices  12.1 us (1%)
    reduce_scatter x1, waiting for transfers between devices, per_device(): lax.psum_scatter(jnp.dot(attn_low, w_proj, preferred_element_type=jnp.flo...  68.6 us
    reduce_scatter x1, waiting for transfers between devices, per_device(): lax.psum_scatter(key_grad_all.astype(jnp.bfloat16), 'ctx', scatter_dimens...  65 us
    all_gather x1, waiting for transfers between devices, per_device(): rows_two = lax.all_gather(normal_two, 'tp', axis=0, tiled=True)  55.7 us
    psum x2, blocking collectives, raise_the_ends(): now = psum(psum(mine, mesh_name), axis_name)  52.7 us
    all_gather x1, waiting for transfers between devices, per_device(): lax.all_gather(grad_resid.astype(jnp.bfloat16), 'tp', axis=0, tiled=True)  52.7 us
    all_gather x1, waiting for transfers between devices, per_device(): grad_rows = lax.all_gather(out_grad, 'tp', axis=0, tiled=True)  48.6 us
    unnamed x15, waiting for transfers between devices  47.3 us
    dynamic_update_slice x8, local copies, waits for them, and re-layouts, grad_step(): lax.dynamic_update_slice_in_dim(key_grad_all, grad_key.reshape(seq_count,...  43.9 us
  transfers between devices with their start and end apart: 15, of which 9 were waited for; matrix products, arithmetic and copies ran while one was open for 19% of the time, Pallas kernels for 0%

profile of v1, /device:TPU:1, one launch (start us, length us, event | category | flops | bytes accessed | tf_op | source)
XLA Modules:
  0.0 1108.7 jit_solution(3416146428077249666)
XLA Ops:
  14.7 30.3 %all-reduce.12 = (bf16[1024]{0:T(1024)(128)(2,1)S(1)}, bf16[128]{0:T(256)(128)(2,1)S(1)}, bf16[128]{0:T(256)(128)(2,1)S(1)}, bf16[1024]{0:T(1024)(128)(2,1)}) all-reduce(bf16[1024]{0:T(1024)(128)(2,1)S(1)} %dynamic-update-slice, bf16[128]{0:T(256)(128)(2,1)S(1)} %dynamic-update-slice.1, ...), channel_id=1, replica_groups=mesh['ctx'=16,'tp'=8] {'ctx'}, use_global_device_ids=true, to_apply=%add.6 | all-reduce | flops 2304 | bytes 9216
  52.0 8.8 gather_fusion.2
  60.9 9.1 gather_fusion.4
  70.9 33.8 %all-gather.9.cloned.1.call-done = bf16[1024,1024]{1,0:T(8,128)(2,1)} async-done(((bf16[128,1024]{1,0:T(8,128)(2,1)}), bf16[1024,1024]{1,0:T(8,128)(2,1)}) %all-gather.9.cloned.1.call-update) | async-done | bytes 2097168 | tf_op jit(solution)/shard_map/all_gather | solution.py:140
  112.1 9.1 gather_fusion.3
  124.0 33.8 %gather_fusion = s32[4096]{0:T(1024)S(1)} fusion(s32[16,2]{0,1:T(2,128)S(1)} %copy-done, s32[4096]{0:T(1024)S(1)} %bitcast.382), kind=kCustom, calls=%fused_computation | custom fusion | bytes 65536 | tf_op jit(solution)/shard_map/gather | solution.py:106
  157.9 15.8 %gather_fusion.1 = s32[4096,4]{1,0:T(8,128)} fusion(s32[4,4096]{0,1:T(8,128)} %copy.155, s32[4096]{0:T(1024)S(1)} %broadcast_clamp_fusion), kind=kCustom, calls=%fused_computation.1 | custom fusion | bytes 147456 | tf_op jit(solution)/shard_map/gather | solution.py:109
  181.5 22.6 %all_gather.49 = bf16[256,1024]{0,1:T(8,128)(2,1)} all-gather(bf16[256,64]{0,1:T(8,128)(2,1)S(1)} %copy-done.40), channel_id=1, replica_groups=mesh['ctx'=16,'tp'=8] {'ctx'}, dimensions={1}, use_global_device_ids=true | all-gather | bytes 557056 | tf_op jit(solution)/shard_map/all_gather | solution.py:135
  213.8 56.3 %while.42 = (s32[]{:T(128)}, f32[4,1,2,256]{3,2,0,1:T(2,128)S(1)}, f32[4,1,2,256]{3,2,0,1:T(2,128)S(1)}, s32[8]{0:T(128)}, s32[4,4096]{1,0:T(4,128)S(1)}, /*inde...) while((s32[]{:T(128)}, f32[4,1,2,256]{3,2,0,1:T(2,128)S(1)}, ...), condition=%wide.wide.region_8.9_spmd.clone, body=%wide.wide.region_5.8_spmd.clone.sunk | while | flops 278407168 | bytes 11155674 | solution.py:189
  270.2 54.3 %while.43 = (s32[]{:T(128)}, f32[4,256,1,2,128]{1,4,3,0,2:T(8,128)S(1)}, s32[8]{0:T(128)}, bf16[4,4096,1,128]{3,1,0,2:T(8,128)(2,1)}, s32[4,4096]{1,0:T(4,128)S(...) while((s32[]{:T(128)}, ...), condition=%wide.wide.region_10.11_spmd.clone, body=%wide.wide.region_9.10_spmd.clone.sunk | while | flops 543162368 | bytes 4767452 | solution.py:210
  328.5 68.6 %reduce-scatter.10.cloned.1.call-done = bf16[128,1024]{1,0:T(8,128)(2,1)} async-done(((bf16[1024,1024]{1,0:T(8,128)(2,1)}), bf16[128,1024]{1,0:T(8,128)(2,1)}) %reduce-scatter.10.cloned.1.call-update) | async-done | bytes 262160 | tf_op jit(solution)/shard_map/reduce_scatter | solution.py:212
  400.8 23.9 %all_gather.53 = bf16[384,1024]{0,1:T(8,128)(2,1)S(1)} all-gather(bf16[384,64]{0,1:T(8,128)(2,1)} %param.34), channel_id=1, replica_groups=mesh['ctx'=16,'tp'=8] {'ctx'}, dimensions={1}, use_global_device_ids=true | all-gather | bytes 835584 | tf_op jit(solution)/shard_map/all_gather | solution.py:221
  424.7 9.1 all-gather.19.cloned.1.call-done
  433.8 55.7 %all-gather.17.cloned.1.call-done = bf16[1024,1024]{1,0:T(8,128)(2,1)} async-done(((bf16[128,1024]{1,0:T(8,128)(2,1)}), bf16[1024,1024]{1,0:T(8,128)(2,1)}) %all-gather.17.cloned.1.call-update) | async-done | bytes 2097168 | tf_op jit(solution)/shard_map/all_gather | solution.py:225
  495.0 48.6 %all-gather.21.cloned.1.call-done = bf16[1024,1024]{1,0:T(8,128)(2,1)} async-done(((bf16[128,1024]{1,0:T(8,128)(2,1)}), bf16[1024,1024]{1,0:T(8,128)(2,1)}) %all-gather.21.cloned.1.call-update) | async-done | bytes 2097168 | tf_op jit(solution)/shard_map/all_gather | solution.py:238
  550.6 29.9 %all_to_all.15 = bf16[8,128,1024]{2,1,0:T(8,128)(2,1)S(1)} all-to-all(bf16[8,128,1024]{2,1,0:T(8,128)(2,1)S(1)} %bitcast.393), channel_id=1, replica_groups=mesh['ctx'=16,'tp'=8] {'tp'}, dimensions={0} | all-to-all | bytes 4194304 | tf_op jit(solution)/shard_map/all_to_all | solution.py:30
  583.4 52.7 %all-gather.23.cloned.1.call-done = bf16[1024,1024]{1,0:T(8,128)(2,1)} async-done(((bf16[128,1024]{1,0:T(8,128)(2,1)}), bf16[1024,1024]{1,0:T(8,128)(2,1)}) %all-gather.23.cloned.1.call-update) | async-done | bytes 2097168 | tf_op jit(solution)/shard_map/all_gather | solution.py:250
  648.6 176.8 %while.44 = (s32[]{:T(128)}, f32[4,256,1,2,128]{1,4,3,0,2:T(8,128)S(1)}, bf16[4,4096,128]{2,1,0:T(8,128)(2,1)}, bf16[4,4096,128]{2,1,0:T(8,128)(2,1)}, s32[8]{0:...) while((s32[]{:T(128)}, ...), condition=%wide.wide.region_18.19_spmd.clone, body=%wide.wide.region_17.18_spmd.clone.sunk | while | flops 1355546624 | bytes 29423888 | solution.py:295
  659.7 5.6 dynamic_update_slice.12
  682.0 5.6 dynamic_update_slice.12
  687.5 5.6 dynamic_update_slice.13
  704.3 5.6 dynamic_update_slice.12
  726.5 5.6 dynamic_update_slice.12
  748.8 5.6 dynamic_update_slice.12
  754.3 5.6 dynamic_update_slice.13
  771.1 5.6 dynamic_update_slice.12
  854.4 41.9 %reduce-scatter.14.cloned.1.call-done = bf16[4,256,128]{2,1,0:T(8,128)(2,1)} async-done(((bf16[4,4096,128]{2,1,0:T(8,128)(2,1)}), bf16[4,256,128]{2,1,0:T(8,128)(2,1)}) %reduce-scatter.14.cloned.1.call-update) | async-done | bytes 262160 | tf_op jit(solution)/shard_map/reduce_scatter | solution.py:302
  897.4 65.0 %reduce-scatter.12.cloned.1.call-done = bf16[4,256,128]{2,1,0:T(8,128)(2,1)} async-done(((bf16[4,4096,128]{2,1,0:T(8,128)(2,1)}), bf16[4,256,128]{2,1,0:T(8,128)(2,1)}) %reduce-scatter.12.cloned.1.call-update) | async-done | bytes 262160 | tf_op jit(solution)/shard_map/reduce_scatter | solution.py:299
  976.5 6.8 all-to-all-start.2
  986.1 45.7 %reduce-scatter.18.cloned.1.call-done = bf16[64,1152]{1,0:T(8,128)(2,1)} async-done(((bf16[1024,1152]{1,0:T(8,128)(2,1)}), bf16[64,1152]{1,0:T(8,128)(2,1)}) %reduce-scatter.18.cloned.1.call-update) | async-done | bytes 147472
  1040.2 31.5 %all-reduce.10 = (f32[1024]{0:T(1024)S(1)}, f32[128]{0:T(128)S(1)}, f32[128]{0:T(128)S(1)}, f32[1024]{0:T(1024)S(1)}) all-reduce(f32[1024]{0:T(1024)S(1)} %get-tuple-element.576, f32[128]{0:T(128)S(1)} %get-tuple-element.574, f32[128]{0:T(128)S(1)} %get-tuple-element.570, ...), channel_id=1, replica_groups=mesh['ctx'=16,'tp'=8] {'ctx'}, use_global_device_ids=true, to_apply=%region_26.27 | all-reduce | flops 2304 | bytes 18432 | tf_op jit(solution)/shard_map/psum | solution.py:16
  1071.8 21.2 %all-reduce.11 = (f32[1024]{0:T(1024)S(1)}, f32[128]{0:T(128)S(1)}, f32[128]{0:T(128)S(1)}, f32[1024]{0:T(1024)S(1)}) all-reduce(f32[1024]{0:T(1024)S(1)} %get-tuple-element.650, f32[128]{0:T(128)S(1)} %get-tuple-element.651, f32[128]{0:T(128)S(1)} %get-tuple-element.652, ...), channel_id=1, replica_groups=mesh['ctx'=16,'tp'=8] {'tp'}, use_global_device_ids=true, to_apply=%region_27.28 | all-reduce | flops 2304 | bytes 18432 | tf_op jit(solution)/shard_map/psum | solution.py:16
  (494 shorter events, 335.6 us)
Async XLA Ops:
  7.2 44.8 %copy-start = (s32[16,2]{0,1:T(2,128)S(1)}, s32[16,2]{0,1:T(2,128)}, u32[]{:S(2)}) copy-start(s32[16,2]{0,1:T(2,128)} %param.22) | copy-start | bytes 388
  7.2 63.7 %all-gather.11.cloned.1.call-start = ((), (), s32[]{:S(2)}) async-start(), calls=%async_computation.9 | async-start | bytes 1114112 | tf_op jit(solution)/shard_map/all_gather | solution.py:132
  8.7 96.0 %all-gather.9.cloned.1.call-start = ((), (), s32[]{:S(2)}) async-start(), calls=%async_computation.8 | async-start | bytes 2359296 | tf_op jit(solution)/shard_map/all_gather | solution.py:140
  49.0 164.8 %all-gather.15.cloned.1.call-start = ((), (), s32[]{:S(2)}) async-start(), calls=%async_computation.11 | async-start | bytes 4456448 | tf_op jit(solution)/shard_map/all_gather | solution.py:157
  49.1 59.0 %copy-start.41 = (f32[128]{0:T(128)}, f32[128]{0:T(128)S(1)}, u32[]{:S(2)}) copy-start(f32[128]{0:T(128)S(1)} %convert_element_type.135) | copy-start | bytes 1540
  70.1 51.2 %copy-start.32 = (s32[1024]{0:T(1024)}, s32[1024]{0:T(1024)S(1)}, u32[]{:S(2)}) copy-start(s32[1024]{0:T(1024)S(1)} %get-tuple-element.1198) | copy-start | bytes 12292
  107.8 99.0 %copy-start.3 = (f32[1024,512]{0,1:T(8,128)}, f32[1024,512]{0,1:T(8,128)S(1)}, u32[]{:S(2)}) copy-start(f32[1024,512]{0,1:T(8,128)S(1)} %fusion.161) | copy-start | bytes 6291460
  112.1 158.1 %all-gather.13.cloned.1.call-start = ((), (), s32[]{:S(2)}) async-start(), calls=%async_computation.10 | async-start | bytes 4456448 | tf_op jit(solution)/shard_map/all_gather | solution.py:158
  121.3 36.5 %copy-start.34 = (s32[1024]{0:T(1024)}, s32[1024]{0:T(1024)S(1)}, u32[]{:S(2)}) copy-start(s32[1024]{0:T(1024)S(1)} %gather_fusion.3) | copy-start | bytes 12292
  157.9 23.6 %copy-start.40 = (bf16[256,64]{0,1:T(8,128)(2,1)S(1)}, bf16[256,64]{0,1:T(8,128)(2,1)}, u32[]{:S(2)}) copy-start(bf16[256,64]{0,1:T(8,128)(2,1)} %param.30) | copy-start | bytes 98308
  213.6 183.5 %reduce-scatter.10.cloned.1.call-start = ((), (), s32[]{:S(2)}) async-start(), calls=%async_computation.12 | async-start | bytes 2359296 | tf_op jit(solution)/shard_map/reduce_scatter | solution.py:212
  213.8 56.3 %copy-start.13 = (f32[4,256,1,2,128]{1,4,3,0,2:T(8,128)S(1)}, f32[4,256,1,2,128]{1,4,3,0,2:T(8,128)}, u32[]{:S(2)}) copy-start(f32[4,256,1,2,128]{1,4,3,0,2:T(8,128)} %custom-call.10) | copy-start | bytes 3145732
  325.5 71.5 %copy-start.5 = (bf16[128,1024]{1,0:T(8,128)(2,1)S(1)}, bf16[128,1024]{1,0:T(8,128)(2,1)}, u32[]{:S(2)}) copy-start(bf16[128,1024]{1,0:T(8,128)(2,1)} %param.21) | copy-start | bytes 786436
  327.7 106.1 %all-gather.19.cloned.1.call-start = ((), (), s32[]{:S(2)}) async-start(), calls=%async_computation.14 | async-start | bytes 1671168 | tf_op jit(solution)/shard_map/all_gather | solution.py:220
  328.4 161.0 %all-gather.17.cloned.1.call-start = ((), (), s32[]{:S(2)}) async-start(), calls=%async_computation.13 | async-start | bytes 2359296 | tf_op jit(solution)/shard_map/all_gather | solution.py:225
  400.0 143.6 %all-gather.21.cloned.1.call-start = ((), (), s32[]{:S(2)}) async-start(), calls=%async_computation.15 | async-start | bytes 2359296 | tf_op jit(solution)/shard_map/all_gather | solution.py:238
  400.8 235.3 %all-gather.23.cloned.1.call-start = ((), (), s32[]{:S(2)}) async-start(), calls=%async_computation.16 | async-start | bytes 2359296 | tf_op jit(solution)/shard_map/all_gather | solution.py:250
  424.7 118.9 %copy-start.24 = (bf16[384,1024]{0,1:T(8,128)(2,1)}, bf16[384,1024]{0,1:T(8,128)(2,1)S(1)}, u32[]{:S(2)}) copy-start(bf16[384,1024]{0,1:T(8,128)(2,1)S(1)} %all_gather.53) | copy-start | bytes 2359300
  582.4 56.8 %copy-start.47 = (f32[128]{0:T(128)}, f32[128]{0:T(128)S(1)}, u32[]{:S(2)}) copy-start(f32[128]{0:T(128)S(1)} %multiply_multiply_fusion.4) | copy-start | bytes 1540
  583.3 313.0 %reduce-scatter.14.cloned.1.call-start = ((), (), s32[]{:S(2)}) async-start(), calls=%async_computation.18 | async-start | bytes 4456448 | tf_op jit(solution)/shard_map/reduce_scatter | solution.py:302
  825.4 137.1 %reduce-scatter.12.cloned.1.call-start = ((), (), s32[]{:S(2)}) async-start(), calls=%async_computation.17 | async-start | bytes 4456448 | tf_op jit(solution)/shard_map/reduce_scatter | solution.py:299
  826.1 205.8 %reduce-scatter.18.cloned.1.call-start = ((), (), s32[]{:S(2)}) async-start(), calls=%async_computation.20 | async-start | bytes 2506752
  840.9 135.6 %all-to-all-start = ((bf16[8,128,1024]{2,1,0:T(8,128)(2,1)}), bf16[8,128,1024]{2,1,0:T(8,128)(2,1)}, u32[]{:S(2)}, u32[]{:S(2)}) async-start(bf16[8,128,1024]{2,1,0:T(8,128)(2,1)} %bitcast.391), calls=%async_computation.1 | async-start | bytes 4194304 | tf_op jit(solution)/shard_map/all_to_all | solution.py:30
  845.3 252.4 %reduce-scatter.16.cloned.1.call-start = ((), (), s32[]{:S(2)}) async-start(), calls=%async_computation.19 | async-start | bytes 1671168
  854.4 111.1 %copy-start.15 = (f32[1024,1,64]{0,2,1:T(8,128)S(1)}, f32[1024,1,64]{0,2,1:T(8,128)}, u32[]{:S(2)}) copy-start(f32[1024,1,64]{0,2,1:T(8,128)} %get-tuple-element.690) | copy-start | bytes 786436
  897.4 69.9 %copy-start.42 = (f32[128]{0:T(128)S(1)}, f32[128]{0:T(128)}, u32[]{:S(2)}) copy-start(f32[128]{0:T(128)} %copy-done.41) | copy-start | bytes 1540
  976.5 62.4 %all-to-all-start.2 = ((bf16[8,128,1024]{2,1,0:T(8,128)(2,1)}), bf16[8,128,1024]{2,1,0:T(8,128)(2,1)S(1)}, u32[]{:S(2)}, u32[]{:S(2)}) async-start(bf16[8,128,1024]{2,1,0:T(8,128)(2,1)} %bitcast.392), calls=%async_computation.5 | async-start | bytes 4194304 | tf_op jit(solution)/shard_map/all_to_all | solution.py:30
  1035.5 59.8 %copy-start.51 = (f32[128]{0:T(128)S(1)}, f32[128]{0:T(128)}, u32[]{:S(2)}) copy-start(f32[128]{0:T(128)} %copy-done.50) | copy-start | bytes 1540
  1035.5 59.8 %copy-start.9 = (f32[128,1024]{1,0:T(8,128)S(1)}, f32[128,1024]{1,0:T(8,128)}, u32[]{:S(2)}) copy-start(f32[128,1024]{1,0:T(8,128)} %copy-done.8) | copy-start | bytes 1572868
  1035.5 59.9 %copy-start.11 = (bf16[128,1024]{1,0:T(8,128)(2,1)S(1)}, bf16[128,1024]{1,0:T(8,128)(2,1)}, u32[]{:S(2)}) copy-start(bf16[128,1024]{1,0:T(8,128)(2,1)} %reduce-scatter.10.cloned.1.call-done) | copy-start | bytes 786436
  1035.5 59.9 %copy-start.17 = (bf16[128,1024]{1,0:T(8,128)(2,1)S(1)}, bf16[128,1024]{1,0:T(8,128)(2,1)}, u32[]{:S(2)}) copy-start(bf16[128,1024]{1,0:T(8,128)(2,1)} %param.35) | copy-start | bytes 786436
  1035.5 59.9 %copy-start.48 = (f32[128]{0:T(128)S(1)}, f32[128]{0:T(128)}, u32[]{:S(2)}) copy-start(f32[128]{0:T(128)} %copy-done.47) | copy-start | bytes 1540
  (45 other events, 111.5 us)
Sparse Core Ops, SparseCore 0:
  10.3 36.2 all-gather.10
  49.5 55.1 all-gather.8
  112.2 36.1 all-gather.14
  213.7 33.6 all-gather.12
  327.8 69.2 reduce-scatter.9
  399.2 34.5 all-gather.18
  436.7 52.6 all-gather.16
  491.8 51.7 all-gather.20
  583.4 52.5 all-gather.22
  825.5 70.7 reduce-scatter.13
  898.7 63.6 reduce-scatter.11
  964.7 67.1 reduce-scatter.17
  1034.3 61.0 reduce-scatter.15
